TPU v7x, 1024 devices: a whole 4x8x16 slice. The times are simulated.
1024 devices in a mesh: uly: 8 (over z_lo, core), blk: 32 (over y, x), dp: 4 (over z_hi).
Axes of the slice: x: 4, y: 8, z: 16 (z_hi: 4, z_lo: 4; z = z_hi * 4 + z_lo), core: 2. Of those that a mesh axis runs over, the one named last changes fastest.
Arguments:
- queries: bfloat16 [4, 4096, 3072], P('dp', 'blk', 'uly'), may hold values from -96 to 96
- keys: bfloat16 [4, 4096, 3072], P('dp', 'blk', 'uly'), may hold values from -6 to 6
- values: bfloat16 [4, 4096, 3072], P('dp', 'blk', 'uly'), may hold values from -6 to 6
- block_lists: int32 [4, 24, 64, 16], P('dp', 'uly', 'blk'), may hold values from 0 to 63, as said below
- block_counts: int32 [4, 24, 64], P('dp', 'uly', 'blk'), may hold values from 1 to 16, as said below
- w_out: bfloat16 [3072, 3072], P('uly', 'dp'), may hold values from -0.875 to 0.875
Outputs:
- mixed: bfloat16 [4, 4096, 3072], P(None, ('blk', 'uly'), 'dp')
Inputs may be any that keep to these rules, and one draw needn't show every extreme that they name: `block_lists`: entry 0 of every list is the query block's own index; the first block_counts entries of a list are distinct; later entries are padding and carry no meaning. `block_counts`: in every clip and head some query block has all 16 entries live.
All inputs are finite; a program needn't handle non-finite values.
Results may differ from a plain program's by a relative error of at most 0.02.
Values may be sent and summed in bfloat16 or wider, within the bound.
A program may use at most 32 MiB of HBM per device.

v0:
```python
import jax
import jax.numpy as jnp
from jax import lax
from jax.sharding import PartitionSpec as P

HD = 128
BLOCK = 64


masked_score = -1e30


def block_allowed_table(chosen, counts_row, total_blocks):
    positions = jnp.arange(chosen.shape[-1])
    usable = positions[None, None, :] < counts_row[:, :, None]
    targets = jnp.arange(total_blocks)
    matches = (chosen[:, :, :, None] == targets[None, None, None, :]) & usable[:, :, :, None]
    return jnp.any(matches, axis=2)


def on_device(queries, keys, values, block_lists, block_counts, w_out):
    row_count = queries.shape[1]
    width_local = queries.shape[2]
    heads_local = width_local // HD
    total_blocks = row_count // BLOCK * lax.axis_size("blk")
    logit_scale_factor = HD ** (-0.5)
    allowed_table = block_allowed_table(block_lists[0], block_counts[0], total_blocks)
    query_heads = queries[0].reshape(row_count, heads_local, HD)
    initial = (
        jnp.full((heads_local, row_count), masked_score, jnp.float32),
        jnp.zeros((heads_local, row_count), jnp.float32),
        jnp.zeros((heads_local, row_count, HD), jnp.float32),
    )
    keys_part = lax.all_gather(keys, "blk", axis=1, tiled=True)
    values_part = lax.all_gather(values, "blk", axis=1, tiled=True)
    key_count = keys_part.shape[1]
    step_len = 512
    keys_steps = keys_part[0].reshape(key_count // step_len, step_len, heads_local, HD)
    values_steps = values_part[0].reshape(key_count // step_len, step_len, heads_local, HD)
    key_starts = step_len * jnp.arange(key_count // step_len, dtype=jnp.int32)

    def sweep_step(current, element):
        keys_heads, values_heads, key_start = element
        peak_old, summed, accumulated = current
        attention_logits = (
            jnp.einsum("qhd,khd->hqk", query_heads, keys_heads, preferred_element_type=jnp.float32)
            * logit_scale_factor
        )
        allowed = lax.dynamic_slice_in_dim(allowed_table, key_start // BLOCK, step_len // BLOCK, 2)
        allowed = jnp.repeat(jnp.repeat(allowed, BLOCK, axis=1), BLOCK, axis=2)
        peak_new = jnp.maximum(
            peak_old, jnp.max(jnp.where(allowed, attention_logits, masked_score), axis=2)
        )
        probabilities = jnp.where(allowed, jnp.exp(attention_logits - peak_new[:, :, None]), 0.0)
        rescale = jnp.exp(peak_old - peak_new)
        summed = summed * rescale + jnp.sum(probabilities, axis=2)
        accumulated = accumulated * rescale[:, :, None] + jnp.einsum(
            "hqk,khd->hqd",
            probabilities.astype(jnp.bfloat16),
            values_heads,
            preferred_element_type=jnp.float32,
        )
        return ((peak_new, summed, accumulated), None)

    finished, unused = lax.scan(sweep_step, initial, (keys_steps, values_steps, key_starts))
    peak, summed, accumulated = finished
    attended = (accumulated / summed[:, :, None]).transpose(1, 0, 2)
    attended = attended.reshape(1, row_count, width_local).astype(jnp.bfloat16)
    partial_sums = jnp.einsum(
        "ctj,jd->ctd",
        lax.all_gather(attended, "dp", axis=0, tiled=True),
        w_out,
        preferred_element_type=jnp.float32,
    )
    return lax.psum_scatter(
        partial_sums.astype(jnp.bfloat16), "uly", scatter_dimension=1, tiled=True
    )


def solution(mesh):
    placed = (
        P("dp", "blk", "uly"),
        P("dp", "blk", "uly"),
        P("dp", "blk", "uly"),
        P("dp", "uly", "blk", None),
        P("dp", "uly", "blk"),
        P("uly", "dp"),
    )
    return jax.shard_map(
        on_device,
        mesh=mesh,
        in_specs=placed,
        out_specs=P(None, ("blk", "uly"), "dp"),
        check_vma=False,
    )
```

profile of v0, /device:TPU:1, one launch (start us, length us, event | category | flops | bytes accessed | tf_op | source)
XLA Modules:
  0.0 350.5 jit_solution(1893800188576512337)
XLA Ops:
  6.5 0.7 all-gather.3.cloned.1.call-update
  7.3 0.7 all-gather.5.cloned.1.call-update
  8.1 1.0 copy.33
  9.1 0.1 copy.37
  9.2 0.8 copy.31
  10.1 0.8 fusion.13
  10.9 101.9 %all-gather.3.cloned.1.call-done = bf16[1,4096,384]{2,1,0:T(8,128)(2,1)} async-done(((bf16[1,128,384]{2,1,0:T(8,128)(2,1)}), bf16[1,4096,384]{2,1,0:T(8,128)(2,1)}) %all-gather.3.cloned.1.call-update) | async-done | bytes 3145744 | tf_op jit(solution)/shard_map/all_gather | solution.py:34
  112.8 9.0 %reshape.37 = bf16[8,512,3,128]{3,2,1,0:T(4,128)(2,1)} reshape(bf16[1,4096,384]{2,1,0:T(8,128)(2,1)} %all-gather.3.cloned.1.call-done) | data formatting | bytes 6291456 | tf_op jit(solution)/shard_map/reshape;squeeze | solution.py:38
  121.8 4.7 %copy.36 = bf16[8,512,3,128]{3,1,2,0:T(8,128)(2,1)} copy(bf16[8,512,3,128]{3,2,1,0:T(4,128)(2,1)} %reshape.37) | data formatting | bytes 6291456
  126.5 83.9 %all-gather.5.cloned.1.call-done = bf16[1,4096,384]{2,1,0:T(8,128)(2,1)} async-done(((bf16[1,128,384]{2,1,0:T(8,128)(2,1)}), bf16[1,4096,384]{2,1,0:T(8,128)(2,1)}) %all-gather.5.cloned.1.call-update) | async-done | bytes 3145744 | tf_op jit(solution)/shard_map/all_gather | solution.py:35
  210.3 9.0 %reshape.38 = bf16[8,512,3,128]{3,2,1,0:T(4,128)(2,1)} reshape(bf16[1,4096,384]{2,1,0:T(8,128)(2,1)} %all-gather.5.cloned.1.call-done) | data formatting | bytes 6291456 | tf_op jit(solution)/shard_map/reshape;squeeze | solution.py:39
  219.3 4.7 %copy.38 = bf16[8,512,3,128]{3,1,2,0:T(8,128)(2,1)} copy(bf16[8,512,3,128]{3,2,1,0:T(4,128)(2,1)} %reshape.38) | data formatting | bytes 6291456
  224.0 51.9 %while.17 = (s32[]{:T(128)}, f32[3,128]{1,0:T(4,128)S(1)}, f32[3,128]{1,0:T(4,128)S(1)}, f32[3,128,128]{2,1,0:T(8,128)S(1)}, s32[8]{0:T(128)S(1)}, /*index=5*/pr...) while((s32[]{:T(128)}, f32[3,128]{1,0:T(4,128)S(1)}, ...), condition=%wide.region_4.5_spmd.clone, body=%wide.region_1.4_spmd.clone.sunk | while | flops 102188944 | bytes 3677265 | solution.py:65
  224.0 0.6 dynamic_slice.48
  227.3 0.1 copy.48
  227.4 0.1 broadcast_in_dim.62
  227.6 1.3 fusion.26
  228.9 0.2 fusion.27
  229.1 1.4 convolution_add_fusion.2
  230.5 0.7 dynamic_slice.48
  233.8 0.1 copy.48
  233.9 0.1 broadcast_in_dim.62
  234.1 1.3 fusion.26
  235.4 0.2 fusion.27
  235.6 1.4 convolution_add_fusion.2
  237.0 0.7 dynamic_slice.48
  240.3 0.1 copy.48
  240.4 0.1 broadcast_in_dim.62
  240.6 1.3 fusion.26
  241.9 0.2 fusion.27
  242.1 1.4 convolution_add_fusion.2
  243.5 0.7 dynamic_slice.48
  246.8 0.1 copy.48
  246.9 0.1 broadcast_in_dim.62
  247.1 1.3 fusion.26
  248.4 0.2 fusion.27
  248.6 1.4 convolution_add_fusion.2
  250.0 0.7 dynamic_slice.48
  253.2 0.1 copy.48
  253.3 0.1 broadcast_in_dim.62
  253.5 1.3 fusion.26
  254.8 0.2 fusion.27
  255.0 1.4 convolution_add_fusion.2
  256.4 0.7 dynamic_slice.48
  259.7 0.1 copy.48
  259.8 0.1 broadcast_in_dim.62
  260.0 1.3 fusion.26
  261.3 0.2 fusion.27
  261.5 1.4 convolution_add_fusion.2
  262.9 0.7 dynamic_slice.48
  266.2 0.1 copy.48
  266.5 1.3 fusion.26
  267.8 0.2 fusion.27
  268.0 1.4 convolution_add_fusion.2
  269.4 0.7 dynamic_slice.48
  272.7 0.1 copy.48
  273.0 1.3 fusion.26
  274.3 0.2 fusion.27
  274.5 1.4 convolution_add_fusion.2
  275.9 0.1 copy.39
  276.1 0.1 copy.40
  276.2 25.5 %all_gather.11 = bf16[4,128,384]{2,1,0:T(8,128)(2,1)S(1)} all-gather(bf16[1,128,384]{2,1,0:T(8,128)(2,1)S(1)} %copy.40), channel_id=1, replica_groups=mesh['uly'=8,'blk'=32,'dp'=4] {'dp'}, dimensions={0}, use_global_device_ids=true | all-gather | bytes 491520 | tf_op jit(solution)/shard_map/all_gather | solution.py:71
  301.6 1.5 convolution_convert_fusion
  303.1 40.8 %reduce-scatter.2.cloned.1.call-done = bf16[4,16,768]{2,1,0:T(8,128)(2,1)} async-done(((bf16[4,128,768]{2,1,0:T(8,128)(2,1)}), bf16[4,16,768]{2,1,0:T(8,128)(2,1)}) %reduce-scatter.2.cloned.1.call-update) | async-done | bytes 98320 | tf_op jit(solution)/shard_map/reduce_scatter | solution.py:75
  (54 shorter events, 1.9 us)
Async XLA Ops:
  6.5 295.1 %copy-start = (bf16[384,768]{1,0:T(8,128)(2,1)S(1)}, bf16[384,768]{1,0:T(8,128)(2,1)}, u32[]{:S(2)}) copy-start(bf16[384,768]{1,0:T(8,128)(2,1)} %param.13) | copy-start | bytes 1769476
  6.5 106.2 %all-gather.3.cloned.1.call-start = ((), (), s32[]{:S(2)}) async-start(), calls=%async_computation.1 | async-start | bytes 3244032 | tf_op jit(solution)/shard_map/all_gather | solution.py:34
  7.3 203.1 %all-gather.5.cloned.1.call-start = ((), (), s32[]{:S(2)}) async-start(), calls=%async_computation.2 | async-start | bytes 3244032 | tf_op jit(solution)/shard_map/all_gather | solution.py:35
  8.0 336.0 %reduce-scatter.2.cloned.1.call-start = ((), (), s32[]{:S(2)}) async-start(), calls=%async_computation.3 | async-start | bytes 884736 | tf_op jit(solution)/shard_map/reduce_scatter | solution.py:75
Sparse Core Ops, SparseCore 0:
  11.7 101.0 all-gather.2
  117.1 93.1 all-gather.4
  303.3 40.6 reduce-scatter.1
where the time goes:
time: 352 us; the launch traced here: 351 us
  waiting for transfers between devices  228 us (65%)
  local copies, waits for them, and re-layouts  37.7 us (11%)
  blocking collectives  25.5 us (7%)
  matrix products  22.7 us (6%)
  loops' own time  20.9 us (6%)
  between operations  13.2 us (4%)
    all_gather x1, waiting for transfers between devices, on_device(): keys_part = lax.all_gather(keys, 'blk', axis=1, tiled=True)  102 us
    all_gather x1, waiting for transfers between devices, on_device(): values_part = lax.all_gather(values, 'blk', axis=1, tiled=True)  83.9 us
    reduce_scatter x1, waiting for transfers between devices, on_device(): lax.psum_scatter(partial_sums.astype(jnp.bfloat16), 'uly', scatter_dimens...  40.8 us
    all_gather x1, blocking collectives, on_device(): lax.all_gather(attended, 'dp', axis=0, tiled=True)  25.5 us
    another operation x1, loops' own time, on_device(): lax.scan(sweep_step, initial, (keys_steps, values_steps, key_starts))  20.9 us
    dot_general x8, matrix products, sweep_step(): jnp.einsum('hqk,khd->hqd', probabilities.astype(jnp.bfloat16), values_hea...  11 us
    unnamed x6, local copies, waits for them, and re-layouts  10.5 us
    dot_general x8, matrix products, sweep_step(): jnp.einsum('qhd,khd->hqk', query_heads, keys_heads, preferred_element_typ...  10.2 us
  transfers between devices with their start and end apart: 3, of which 3 were waited for; matrix products, arithmetic and copies ran while one was open for 5% of the time, Pallas kernels for 0%

commit v1 on v0

v1 whole, which is shorter than its diff:
```python
import functools
import math

import jax
import jax.numpy as jnp
from jax import lax
from jax.experimental import pallas as pl
from jax.experimental.pallas import tpu as pltpu
from jax.sharding import PartitionSpec as P

HD = 128
BLOCK = 64
X_SIZE = 4
MASKED = -1e30
SCALE = HD**-0.5 * math.log2(math.e)
MESH = pl.DeviceIdType.MESH
F32 = jnp.float32
BF16 = jnp.bfloat16


def fused(
    sizes,
    q_hbm,
    k_hbm,
    v_hbm,
    lists,
    counts,
    w_hbm,
    out,
    q_all,
    t_all,
    t_wide,
    hot,
    k_all,
    v_all,
    v_stage,
    top_now,
    sum_now,
    acc,
    o_own,
    o_out,
    o_in,
    st_out,
    st_in,
    a_out,
    a_all,
    w_all,
    part,
    r_out,
    r_in,
    load_sem,
    kv_send,
    kv_recv,
    q_send,
    q_recv,
    t_send,
    t_recv,
    o_send,
    o_recv,
    st_send,
    st_recv,
    a_send,
    a_recv,
    w_send,
    w_recv,
    r_send,
    r_recv,
):
    nx, ny, nz, nd = sizes
    heads, rows = q_hbm.shape[2] // HD, q_hbm.shape[1]
    take = rows // (2 * nz)
    far = ny // 2
    u, b, d = lax.axis_index("uly"), lax.axis_index("blk"), lax.axis_index("dp")
    z, core = u // 2, u % 2
    y, x = b // nx, b % nx

    def at_y(step):
        return {"blk": lax.rem(y + step + ny, ny) * nx + x}

    def at_x(step):
        return {"blk": y * nx + lax.rem(x + step + nx, nx)}

    def at_z(step):
        return {"uly": lax.rem(z + step + nz, nz) * 2 + core}

    def at_a(flip, step):
        return {
            "uly": z * 2 + lax.rem(core + flip, 2),
            "dp": lax.rem(d + step + nd, nd),
        }

    def send(src, dst, send_sem, recv_sem, device):
        return pltpu.make_async_remote_copy(
            src_ref=src,
            dst_ref=dst,
            send_sem=send_sem,
            recv_sem=recv_sem,
            device_id=device,
            device_id_type=MESH,
        )

    def kv_copy(h, way, step, which):
        buffer = (k_all, v_all)[which]
        old, new = (step - 1, step) if way == 0 else ((ny - step + 1) % ny, ny - step)
        return send(
            buffer.at[h, old],
            buffer.at[h, new],
            kv_send.at[h, way, step - 1, which],
            kv_recv.at[h, new, which],
            at_y(1 - 2 * way),
        )

    def q_copy(h, j):
        return send(
            q_all.at[h, 0], q_all.at[h, j], q_send.at[h, j], q_recv.at[h, j], at_x(j)
        )

    def t_copy(j):
        return send(t_all.at[0], t_all.at[j], t_send.at[j], t_recv.at[j], at_x(j))

    def o_copy(h, j):
        return send(
            o_out.at[h, j], o_in.at[h, j], o_send.at[h, j], o_recv.at[h, j], at_x(-j)
        )

    def st_copy(h, j):
        return send(
            st_out.at[h, j],
            st_in.at[h, j],
            st_send.at[h, j],
            st_recv.at[h, j],
            at_x(-j),
        )

    def a_copy(h, flip, step):
        return send(
            a_out.at[h, lax.rem(core + flip, 2)],
            a_all.at[h, step, :, pl.ds(flip * HD, HD)],
            a_send.at[h, flip, step],
            a_recv.at[h, flip, step],
            at_a(flip, step),
        )

    def w_copy(h):
        return send(
            w_hbm.at[pl.ds(h * HD, HD), :],
            w_all.at[h, pl.ds(HD, HD), :],
            w_send.at[h],
            w_recv.at[h],
            at_a(1, 0),
        )

    def r_copy(j, step):
        return send(
            r_out.at[j, step],
            r_in.at[j, step],
            r_send.at[j, step],
            r_recv.at[j, step],
            at_z(j),
        )

    started = []

    def start(copy):
        copy.start()
        started.append(copy)

    def ways(step):
        pairs = []
        for which in range(2):
            for way in range(2):
                if step < far or which == way:
                    pairs.append((way, which))
        return pairs

    def load(src, dst, sem):
        copy = pltpu.make_async_copy(src, dst, sem)
        copy.start()
        return copy

    load_k = [
        load(k_hbm.at[0, :, pl.ds(h * HD, HD)], k_all.at[h, 0], load_sem.at[0, h])
        for h in range(heads)
    ]
    load_v = [
        load(v_hbm.at[0, :, pl.ds(h * HD, HD)], v_stage.at[h], load_sem.at[1, h])
        for h in range(heads)
    ]
    load_q = [
        load(q_hbm.at[0, :, pl.ds(h * HD, HD)], q_all.at[h, 0], load_sem.at[2, h])
        for h in range(heads)
    ]
    load_w = [
        load(
            w_hbm.at[pl.ds(h * HD, HD), :],
            w_all.at[h, pl.ds(0, HD), :],
            load_sem.at[3, h],
        )
        for h in range(heads)
    ]

    barrier = pltpu.get_barrier_semaphore()
    around = [at_y(1), at_y(-1)]
    around += [at_x(j) for j in range(1, nx)]
    around += [at_a(f, s) for s in range(nd) for f in range(2) if f or s]
    around += [at_z(j) for j in range(1, nz)]
    for device in around:
        pl.semaphore_signal(barrier, inc=1, device_id=device, device_id_type=MESH)

    lane = lax.broadcasted_iota(jnp.int32, (1, HD), 1)
    for h in range(heads):
        for i in range(rows // BLOCK):
            seen = jnp.zeros((1, HD), jnp.int32)
            live = counts[0, h, i]
            for n in range(lists.shape[3]):
                hit = (lane == lists[0, h, i, n]) & (jnp.full((1, HD), n) < live)
                seen = seen | hit.astype(jnp.int32)
            line = h * (rows // BLOCK) + i
            t_all[0, line : line + 1, :] = jnp.where(seen > 0, 0.0, MASKED)

    for copy in load_k:
        copy.wait()
    load_v[0].wait()
    v_all[0, 0] = v_stage[0].T
    load_q[0].wait()
    pl.semaphore_wait(barrier, len(around))

    for way, which in ways(1):
        start(kv_copy(0, way, 1, which))
    for j in range(1, nx):
        start(t_copy(j))
        start(q_copy(0, j))

    row = lax.broadcasted_iota(jnp.int32, (rows, HD), 0)
    column = lax.broadcasted_iota(jnp.int32, (rows, HD), 1)
    per = rows // BLOCK
    for s in range(ny):
        owner = lax.rem(y - s + ny, ny) * nx + x
        hot[s] = jnp.where(column == owner * per + row // BLOCK, 1.0, 0.0).astype(BF16)

    for h in range(1, heads):
        load_v[h].wait()
        v_all[h, 0] = v_stage[h].T
        load_q[h].wait()
        for j in range(1, nx):
            start(q_copy(h, j))
    for h in range(heads):
        start(w_copy(h))

    for j in range(1, nx):
        t_copy(j).wait_recv()
    for h in range(heads):
        for j in range(nx):
            for i in range(per):
                line = h * per + i
                wide = jnp.broadcast_to(t_all[j, line : line + 1, :], (BLOCK, HD))
                t_wide[h, j, i * BLOCK : (i + 1) * BLOCK, :] = wide.astype(BF16)

    def attend(h, slots, first):
        keys = jnp.concatenate(
            [jnp.concatenate([k_all[h, s], hot[s]], axis=1) for s in slots], axis=0
        )
        values = jnp.concatenate([v_all[h, s] for s in slots], axis=1)
        queries = jnp.concatenate(
            [q_all[h].reshape(nx * rows, HD), t_wide[h].reshape(nx * rows, HD)], axis=1
        )
        scores = lax.dot_general(
            keys, queries, (((1,), (1,)), ((), ())), preferred_element_type=F32
        )
        top = jnp.max(scores, axis=0, keepdims=True)
        if not first:
            old = top_now[...]
            top = jnp.maximum(top, old)
        probs = jnp.exp2((scores - top) * SCALE)
        total = jnp.sum(probs, axis=0, keepdims=True)
        mixed = jnp.dot(values, probs.astype(BF16), preferred_element_type=F32)
        if not first:
            fade = jnp.exp2((old - top) * SCALE)
            total = total + sum_now[...] * fade
            mixed = mixed + acc[...] * fade
        top_now[...] = top
        sum_now[...] = total
        acc[...] = mixed

    def share(h):
        for j in range(nx):
            lanes = slice(j * rows, (j + 1) * rows)
            st_out[h, j, 0:1, :] = top_now[:, lanes]
            st_out[h, j, 1:2, :] = sum_now[:, lanes]
            if j == 0:
                o_own[h] = acc[:, lanes]
            else:
                o_out[h, j] = acc[:, lanes].astype(BF16)
                start(st_copy(h, j))
                start(o_copy(h, j))

    def merge(h):
        for j in range(1, nx):
            st_copy(h, j).wait_recv()
        tops = [st_out[h, 0, 0:1, :]] + [st_in[h, j, 0:1, :] for j in range(1, nx)]
        sums = [st_out[h, 0, 1:2, :]] + [st_in[h, j, 1:2, :] for j in range(1, nx)]
        top = functools.reduce(jnp.maximum, tops)
        weights = [jnp.exp2((t - top) * SCALE) for t in tops]
        denom = sum(w * s for w, s in zip(weights, sums))
        total = o_own[h] * weights[0]
        for j in range(1, nx):
            o_copy(h, j).wait_recv()
            total = total + o_in[h, j].astype(F32) * weights[j]
        attended = (total / denom).T.astype(BF16)
        for i in range(2 * nz):
            place = slice(i // 2 * take, (i // 2 + 1) * take)
            a_out[h, i % 2, place, :] = attended[i * take : (i + 1) * take, :]
        for step in range(nd - 1, -1, -1):
            for flip in range(2):
                if flip or step:
                    start(a_copy(h, flip, step))
        a_all[h, 0, :, 0:HD] = a_out[h, core]

    def project(h, steps):
        for step in steps:
            for flip in range(2):
                if flip or step:
                    a_copy(h, flip, step).wait_recv()
        group = len(steps)
        lines = group * nz * take
        rows_in = a_all[h, steps[0] : steps[0] + group].reshape(lines, 2 * HD)
        more = jnp.dot(rows_in, w_all[h], preferred_element_type=F32)
        more = more.reshape(group, nz, take, more.shape[1])
        if h > 0:
            more = more + part[steps[0] : steps[0] + group]
        part[steps[0] : steps[0] + group] = more

    for h in range(heads):
        for j in range(1, nx):
            q_copy(h, j).wait_recv()
        attend(h, [0], True)
        for step in range(1, far):
            for way, which in ways(step):
                kv_copy(h, way, step, which).wait_recv()
                if (way, which) in ways(step + 1):
                    start(kv_copy(h, way, step + 1, which))
            if step == 1 and h + 1 < heads:
                for way, which in ways(1):
                    start(kv_copy(h + 1, way, 1, which))
            attend(h, [step, ny - step], False)
            if step == max(1, far - 2) and h > 0:
                merge(h - 1)
            if h == 2 and step == far - 1:
                for i in range(heads):
                    load_w[i].wait()
                    w_copy(i).wait_recv()
                project(0, list(range(nd)))
        for way, which in ways(far):
            kv_copy(h, way, far, which).wait_recv()
        attend(h, [far], False)
        share(h)

    last = heads - 1
    merge(last)
    for h in range(1, last):
        project(h, list(range(nd)))
    for step in range(nd):
        project(last, [step])
        for j in range(1, nz):
            goal = lax.rem(z + j, nz)
            r_out[j, step] = part[step, goal].astype(BF16)
            start(r_copy(j, step))
    for step in range(nd):
        total = part[step, z]
        for j in range(1, nz):
            r_copy(j, step).wait_recv()
            total = total + r_in[j, step].astype(F32)
        out[lax.rem(d - step + nd, nd)] = total.astype(BF16)

    for copy in started:
        copy.wait_send()


def on_device(sizes, queries, keys, values, block_lists, block_counts, w_out):
    nx, ny, nz, nd = sizes
    rows, heads = queries.shape[1], queries.shape[2] // HD
    take, width = rows // (2 * nz), w_out.shape[1]
    dma = pltpu.SemaphoreType.DMA
    far = ny // 2
    return pl.pallas_call(
        functools.partial(fused, sizes),
        out_shape=jax.ShapeDtypeStruct((nd, take, width), BF16),
        in_specs=[pl.BlockSpec(memory_space=pl.ANY)] * 3
        + [pl.BlockSpec(memory_space=pltpu.SMEM)] * 2
        + [pl.BlockSpec(memory_space=pl.ANY)],
        out_specs=pl.BlockSpec(memory_space=pltpu.VMEM),
        scratch_shapes=[
            pltpu.VMEM((heads, nx, rows, HD), BF16),
            pltpu.VMEM((nx, 8, HD), F32),
            pltpu.VMEM((heads, nx, rows, HD), BF16),
            pltpu.VMEM((ny, rows, HD), BF16),
            pltpu.VMEM((heads, ny, rows, HD), BF16),
            pltpu.VMEM((heads, ny, HD, rows), BF16),
            pltpu.VMEM((heads, rows, HD), BF16),
            pltpu.VMEM((1, nx * rows), F32),
            pltpu.VMEM((1, nx * rows), F32),
            pltpu.VMEM((HD, nx * rows), F32),
            pltpu.VMEM((heads, HD, rows), F32),
            pltpu.VMEM((heads, nx, HD, rows), BF16),
            pltpu.VMEM((heads, nx, HD, rows), BF16),
            pltpu.VMEM((heads, nx, 8, rows), F32),
            pltpu.VMEM((heads, nx, 8, rows), F32),
            pltpu.VMEM((heads, 2, nz * take, HD), BF16),
            pltpu.VMEM((heads, nd, nz * take, 2 * HD), BF16),
            pltpu.VMEM((heads, 2 * HD, width), BF16),
            pltpu.VMEM((nd, nz, take, width), F32),
            pltpu.VMEM((nz, nd, take, width), BF16),
            pltpu.VMEM((nz, nd, take, width), BF16),
            dma((4, heads)),
            dma((heads, 2, far, 2)),
            dma((heads, ny, 2)),
            dma((heads, nx)),
            dma((heads, nx)),
            dma((nx,)),
            dma((nx,)),
            dma((heads, nx)),
            dma((heads, nx)),
            dma((heads, nx)),
            dma((heads, nx)),
            dma((heads, 2, nd)),
            dma((heads, 2, nd)),
            dma((heads,)),
            dma((heads,)),
            dma((nz, nd)),
            dma((nz, nd)),
        ],
        compiler_params=pltpu.CompilerParams(
            collective_id=0, has_side_effects=True, vmem_limit_bytes=40 * 2**20
        ),
        name="attention",
    )(queries, keys, values, block_lists, block_counts, w_out)


def solution(mesh):
    shape = mesh.shape
    sizes = (X_SIZE, shape["blk"] // X_SIZE, shape["uly"] // 2, shape["dp"])
    placed = (
        P("dp", "blk", "uly"),
        P("dp", "blk", "uly"),
        P("dp", "blk", "uly"),
        P("dp", "uly", "blk", None),
        P("dp", "uly", "blk"),
        P("uly", "dp"),
    )
    return jax.shard_map(
        functools.partial(on_device, sizes),
        mesh=mesh,
        in_specs=placed,
        out_specs=P(None, ("blk", "uly"), "dp"),
        check_vma=False,
    )
```

time: 352 us -> 88 us (0.25)
  waiting for transfers between devices: 228 us -> 0 us
  Pallas kernels: 0 us -> 82.6 us
  local copies, waits for them, and re-layouts: 37.7 us -> 5.17 us
  blocking collectives: 25.5 us -> 0 us
  matrix products: 22.7 us -> 0 us
  loops' own time: 20.9 us -> 0 us
  between operations: 13.2 us -> 0.01 us
    all_gather x2 -> x0, waiting for transfers between devices: 186 us -> none  [the longest x1 102 us: on_device(): keys_part = lax.all_gather(keys, 'blk', axis=1, tiled=True)]
    pallas_call x0 -> x1, Pallas kernels: none -> 82.6 us  [on_device(): pl.pallas_call(functools.partial(fused, sizes), out_shape=jax.ShapeDtypeS...]
    reduce_scatter x1 -> x0, waiting for transfers between devices: 40.8 us -> none  [on_device(): lax.psum_scatter(partial_sums.astype(jnp.bfloat16), 'uly', scatter_dimens...]
    all_gather x1 -> x0, blocking collectives: 25.5 us -> none  [on_device(): lax.all_gather(attended, 'dp', axis=0, tiled=True)]
    dot_general x17 -> x0, matrix products: 22.7 us -> none  [the longest x8 11 us: sweep_step(): jnp.einsum('hqk,khd->hqd', probabilities.astype(jnp.bfloat16), values_hea...]
    another operation x1 -> x0, loops' own time: 20.9 us -> none  [on_device(): lax.scan(sweep_step, initial, (keys_steps, values_steps, key_starts))]
    another operation x2 -> x0, local copies, waits for them, and re-layouts: 18 us -> none  [the longest x1 9 us: on_device(): keys_part[0].reshape(key_count // step_len, step_len, heads_local, HD)]
    dynamic_slice x24 -> x0, local copies, waits for them, and re-layouts: 6.69 us -> none  [the longest x8 5.2 us: on_device(): lax.scan(sweep_step, initial, (keys_steps, values_steps, key_starts))]
  transfers between devices with their start and end apart: 3 -> 0, of which waited for: 3 -> 0; matrix products, arithmetic and copies ran while one was open for 5% -> 0% of each run, Pallas kernels for 0% -> 0%
where the time goes in v1:
time: 88 us; the launch traced here: 87.7 us
  Pallas kernels  82.6 us (94%)
  local copies, waits for them, and re-layouts  5.17 us (6%)
    pallas_call x1, Pallas kernels, on_device(): pl.pallas_call(functools.partial(fused, sizes), out_shape=jax.ShapeDtypeS...  82.6 us
    unnamed x12, local copies, waits for them, and re-layouts  5.17 us

profile of v1, /device:TPU:1, one launch (start us, length us, event | category | flops | bytes accessed | tf_op | source)
XLA Modules:
  0.0 87.7 jit_solution(1236674360376668908)
XLA Ops:
  0.0 0.0 copy-start.4
  0.0 0.8 copy.7.counts
  0.8 0.0 copy-done.4
  0.8 0.0 copy-start
  0.8 1.1 %copy-done = bf16[384,768]{1,0:T(8,128)(2,1)S(1)} copy-done((bf16[384,768]{1,0:T(8,128)(2,1)S(1)}, bf16[384,768]{1,0:T(8,128)(2,1)}, u32[]{:S(2)}) %copy-start) | copy-done | bytes 589848
  1.8 0.0 copy-start.1
  1.9 0.9 %copy-done.1 = bf16[1,128,384]{2,1,0:T(8,128)(2,1)S(1)} copy-done((bf16[1,128,384]{2,1,0:T(8,128)(2,1)S(1)}, bf16[1,128,384]{2,1,0:T(8,128)(2,1)}, u32[]{:S(2)}) %copy-start.1) | copy-done | bytes 98328
  2.7 0.0 copy-start.2
  2.7 0.9 %copy-done.2 = bf16[1,128,384]{2,1,0:T(8,128)(2,1)S(1)} copy-done((bf16[1,128,384]{2,1,0:T(8,128)(2,1)S(1)}, bf16[1,128,384]{2,1,0:T(8,128)(2,1)}, u32[]{:S(2)}) %copy-start.2) | copy-done | bytes 98328
  3.6 0.0 copy-start.3
  3.6 0.9 %copy-done.3 = bf16[1,128,384]{2,1,0:T(8,128)(2,1)S(1)} copy-done((bf16[1,128,384]{2,1,0:T(8,128)(2,1)S(1)}, bf16[1,128,384]{2,1,0:T(8,128)(2,1)}, u32[]{:S(2)}) %copy-start.3) | copy-done | bytes 98328
  4.5 82.6 %attention.1 = bf16[4,16,768]{2,1,0:T(8,128)(2,1)S(1)} custom-call(bf16[1,128,384]{2,1,0:T(8,128)(2,1)S(1)} %copy-done.1, bf16[1,128,384]{2,1,0:T(8,128)(2,1)S(1)} %copy-done.2, bf16[1,128,384]{2,1,0:T(8,128)(2,1)S(1)} %copy-done.3, s32[1,3,2,16]{3,2,1,0:T(2,128)S(1)} %copy-done.4, s32[1,3,2]{2,1,0:T(4,128)S(1)} %copy.7.counts, bf16[384,768]{1,0:T(8,128)(2,1)S(1)} %copy-done), custom_call_target="tpu_custom_call" | custom-call | tf_op jit(solution)/shard_map/attention/pallas_call | solution.py:385
  87.1 0.6 copy.9
Async XLA Ops:
  0.0 0.8 copy-start.4
  0.8 1.1 %copy-start = (bf16[384,768]{1,0:T(8,128)(2,1)S(1)}, bf16[384,768]{1,0:T(8,128)(2,1)}, u32[]{:S(2)}) copy-start(bf16[384,768]{1,0:T(8,128)(2,1)} %w_hbm.1) | copy-start | bytes 1769476
  1.8 0.9 %copy-start.1 = (bf16[1,128,384]{2,1,0:T(8,128)(2,1)S(1)}, bf16[1,128,384]{2,1,0:T(8,128)(2,1)}, u32[]{:S(2)}) copy-start(bf16[1,128,384]{2,1,0:T(8,128)(2,1)} %q_hbm.1) | copy-start | bytes 294916
  2.7 0.9 %copy-start.2 = (bf16[1,128,384]{2,1,0:T(8,128)(2,1)S(1)}, bf16[1,128,384]{2,1,0:T(8,128)(2,1)}, u32[]{:S(2)}) copy-start(bf16[1,128,384]{2,1,0:T(8,128)(2,1)} %k_hbm.1) | copy-start | bytes 294916
  3.6 0.9 %copy-start.3 = (bf16[1,128,384]{2,1,0:T(8,128)(2,1)S(1)}, bf16[1,128,384]{2,1,0:T(8,128)(2,1)}, u32[]{:S(2)}) copy-start(bf16[1,128,384]{2,1,0:T(8,128)(2,1)} %v_hbm.1) | copy-start | bytes 294916

commit v2 on v1

--- a/solution.py
+++ b/solution.py
@@ -141,6 +141,17 @@
             at_a(flip, step),
         )
 
+    def a_relay(h, flip):
+        old = 1 if flip == 0 else nd - 1
+        lanes = pl.ds(flip * HD, HD)
+        return send(
+            a_all.at[h, old, :, lanes],
+            a_all.at[h, 2, :, lanes],
+            a_send.at[h, flip, 2],
+            a_recv.at[h, flip, 2],
+            at_a(0, 1 if flip == 0 else -1),
+        )
+
     def w_copy(h):
         return send(
             w_hbm.at[pl.ds(h * HD, HD), :],
@@ -202,7 +213,8 @@
     barrier = pltpu.get_barrier_semaphore()
     around = [at_y(1), at_y(-1)]
     around += [at_x(j) for j in range(1, nx)]
-    around += [at_a(f, s) for s in range(nd) for f in range(2) if f or s]
+    near = sorted({1 % nd, nd - 1} - {0})
+    around += [at_a(f, s) for s in [0] + near for f in range(2) if f or s]
     around += [at_z(j) for j in range(1, nz)]
     for device in around:
         pl.semaphore_signal(barrier, inc=1, device_id=device, device_id_type=MESH)
@@ -211,7 +223,7 @@
     for h in range(heads):
         for i in range(rows // BLOCK):
             seen = jnp.zeros((1, HD), jnp.int32)
-            live = counts[0, h, i]
+            live = counts[0, i, h]
             for n in range(lists.shape[3]):
                 hit = (lane == lists[0, h, i, n]) & (jnp.full((1, HD), n) < live)
                 seen = seen | hit.astype(jnp.int32)
@@ -227,6 +239,10 @@
 
     for way, which in ways(1):
         start(kv_copy(0, way, 1, which))
+    load_v[1].wait()
+    v_all[1, 0] = v_stage[1].T
+    for way, which in ways(1):
+        start(kv_copy(1, way, 1, which))
     for j in range(1, nx):
         start(t_copy(j))
         start(q_copy(0, j))
@@ -239,8 +255,9 @@
         hot[s] = jnp.where(column == owner * per + row // BLOCK, 1.0, 0.0).astype(BF16)
 
     for h in range(1, heads):
-        load_v[h].wait()
-        v_all[h, 0] = v_stage[h].T
+        if h > 1:
+            load_v[h].wait()
+            v_all[h, 0] = v_stage[h].T
         load_q[h].wait()
         for j in range(1, nx):
             start(q_copy(h, j))
@@ -269,28 +286,28 @@
         )
         top = jnp.max(scores, axis=0, keepdims=True)
         if not first:
-            old = top_now[...]
+            old = top_now[h]
             top = jnp.maximum(top, old)
         probs = jnp.exp2((scores - top) * SCALE)
         total = jnp.sum(probs, axis=0, keepdims=True)
         mixed = jnp.dot(values, probs.astype(BF16), preferred_element_type=F32)
         if not first:
             fade = jnp.exp2((old - top) * SCALE)
-            total = total + sum_now[...] * fade
-            mixed = mixed + acc[...] * fade
-        top_now[...] = top
-        sum_now[...] = total
-        acc[...] = mixed
+            total = total + sum_now[h] * fade
+            mixed = mixed + acc[h] * fade
+        top_now[h] = top
+        sum_now[h] = total
+        acc[h] = mixed
 
     def share(h):
         for j in range(nx):
             lanes = slice(j * rows, (j + 1) * rows)
-            st_out[h, j, 0:1, :] = top_now[:, lanes]
-            st_out[h, j, 1:2, :] = sum_now[:, lanes]
+            st_out[h, j, 0:1, :] = top_now[h, :, lanes]
+            st_out[h, j, 1:2, :] = sum_now[h, :, lanes]
             if j == 0:
-                o_own[h] = acc[:, lanes]
+                o_own[h] = acc[h, :, lanes]
             else:
-                o_out[h, j] = acc[:, lanes].astype(BF16)
+                o_out[h, j] = acc[h, :, lanes].astype(BF16)
                 start(st_copy(h, j))
                 start(o_copy(h, j))
 
@@ -310,57 +327,65 @@
         for i in range(2 * nz):
             place = slice(i // 2 * take, (i // 2 + 1) * take)
             a_out[h, i % 2, place, :] = attended[i * take : (i + 1) * take, :]
-        for step in range(nd - 1, -1, -1):
+        for step in near + [0]:
             for flip in range(2):
                 if flip or step:
                     start(a_copy(h, flip, step))
         a_all[h, 0, :, 0:HD] = a_out[h, core]
 
-    def project(h, steps):
-        for step in steps:
+    arrived = set()
+
+    def receive(h, flip, step):
+        if (flip or step) and (h, flip, step) not in arrived:
+            arrived.add((h, flip, step))
+            a_copy(h, flip, step).wait_recv()
+
+    def relay(h):
+        if nd > 3:
             for flip in range(2):
-                if flip or step:
-                    a_copy(h, flip, step).wait_recv()
-        group = len(steps)
-        lines = group * nz * take
-        rows_in = a_all[h, steps[0] : steps[0] + group].reshape(lines, 2 * HD)
-        more = jnp.dot(rows_in, w_all[h], preferred_element_type=F32)
-        more = more.reshape(group, nz, take, more.shape[1])
-        if h > 0:
-            more = more + part[steps[0] : steps[0] + group]
-        part[steps[0] : steps[0] + group] = more
-
+                receive(h, flip, 1 if flip == 0 else nd - 1)
+                start(a_relay(h, flip))
+
+    def receive_keys(h, step):
+        for way, which in ways(step):
+            kv_copy(h, way, step, which).wait_recv()
+            if step < far and (way, which) in ways(step + 1):
+                start(kv_copy(h, way, step + 1, which))
+
+    last = heads - 1
+    events = sorted((h + step, -h, step) for h in range(heads) for step in range(1, far + 1))
+    for _, h, step in events:
+        h = -h
+        receive_keys(h, step)
+        if step == 1:
+            if h + 2 < heads:
+                for way, which in ways(1):
+                    start(kv_copy(h + 2, way, 1, which))
+            for j in range(1, nx):
+                q_copy(h, j).wait_recv()
+        slots = [0] * (step == 1) + ([step, ny - step] if step < far else [far])
+        attend(h, slots, step == 1)
+        if step == far:
+            share(h)
+        if (h, step) == (last, far - 1):
+            merge(0)
+    for h in range(1, heads):
+        merge(h)
     for h in range(heads):
-        for j in range(1, nx):
-            q_copy(h, j).wait_recv()
-        attend(h, [0], True)
-        for step in range(1, far):
-            for way, which in ways(step):
-                kv_copy(h, way, step, which).wait_recv()
-                if (way, which) in ways(step + 1):
-                    start(kv_copy(h, way, step + 1, which))
-            if step == 1 and h + 1 < heads:
-                for way, which in ways(1):
-                    start(kv_copy(h + 1, way, 1, which))
-            attend(h, [step, ny - step], False)
-            if step == max(1, far - 2) and h > 0:
-                merge(h - 1)
-            if h == 2 and step == far - 1:
-                for i in range(heads):
-                    load_w[i].wait()
-                    w_copy(i).wait_recv()
-                project(0, list(range(nd)))
-        for way, which in ways(far):
-            kv_copy(h, way, far, which).wait_recv()
-        attend(h, [far], False)
-        share(h)
-
-    last = heads - 1
-    merge(last)
-    for h in range(1, last):
-        project(h, list(range(nd)))
-    for step in range(nd):
-        project(last, [step])
+        relay(h)
+    for h in range(heads):
+        load_w[h].wait()
+        w_copy(h).wait_recv()
+
+    lines, depth = nz * take, heads * 2 * HD
+    weights = w_all[...].reshape(depth, w_all.shape[2])
+    for step in [0] + near + list(range(2, nd - 1)):
+        for h in range(heads):
+            for flip in range(2):
+                receive(h, flip, step)
+        rows_in = jnp.concatenate([a_all[h, step] for h in range(heads)], axis=1)
+        mixed = jnp.dot(rows_in, weights, preferred_element_type=F32)
+        part[step] = mixed.reshape(nz, take, mixed.shape[1])
         for j in range(1, nz):
             goal = lax.rem(z + j, nz)
             r_out[j, step] = part[step, goal].astype(BF16)
@@ -397,9 +422,9 @@
             pltpu.VMEM((heads, ny, rows, HD), BF16),
             pltpu.VMEM((heads, ny, HD, rows), BF16),
             pltpu.VMEM((heads, rows, HD), BF16),
-            pltpu.VMEM((1, nx * rows), F32),
-            pltpu.VMEM((1, nx * rows), F32),
-            pltpu.VMEM((HD, nx * rows), F32),
+            pltpu.VMEM((heads, 1, nx * rows), F32),
+            pltpu.VMEM((heads, 1, nx * rows), F32),
+            pltpu.VMEM((heads, HD, nx * rows), F32),
             pltpu.VMEM((heads, HD, rows), F32),
             pltpu.VMEM((heads, nx, HD, rows), BF16),
             pltpu.VMEM((heads, nx, HD, rows), BF16),
@@ -430,10 +455,10 @@
             dma((nz, nd)),
         ],
         compiler_params=pltpu.CompilerParams(
-            collective_id=0, has_side_effects=True, vmem_limit_bytes=40 * 2**20
+            collective_id=0, has_side_effects=True, vmem_limit_bytes=60 * 2**20
         ),
         name="attention",
-    )(queries, keys, values, block_lists, block_counts, w_out)
+    )(queries, keys, values, block_lists, block_counts.transpose(0, 2, 1), w_out)
 
 
 def solution(mesh):

time: 88 us -> 70.3 us (0.80)
  Pallas kernels: 82.6 us -> 68.6 us
  local copies, waits for them, and re-layouts: 5.17 us -> 1.54 us
    pallas_call x1, Pallas kernels: 82.6 us -> 68.6 us  [on_device(): pl.pallas_call(functools.partial(fused, sizes), out_shape=jax.ShapeDtypeS...]
    unnamed x12 -> x1, local copies, waits for them, and re-layouts: 5.17 us -> 1.54 us
where the time goes in v2:
time: 70.3 us; the launch traced here: 70.1 us
  Pallas kernels  68.6 us (98%)
  local copies, waits for them, and re-layouts  1.54 us (2%)
    pallas_call x1, Pallas kernels, on_device(): pl.pallas_call(functools.partial(fused, sizes), out_shape=jax.ShapeDtypeS...  68.6 us
    unnamed x1, local copies, waits for them, and re-layouts  1.54 us

profile of v2, /device:TPU:1, one launch (start us, length us, event | category | flops | bytes accessed | tf_op | source)
XLA Modules:
  0.0 70.1 jit_solution(10246578708634836096)
XLA Ops:
  0.0 68.6 %attention.1 = bf16[4,16,768]{2,1,0:T(8,128)(2,1)} custom-call(bf16[1,128,384]{2,1,0:T(8,128)(2,1)} %q_hbm.1, bf16[1,128,384]{2,1,0:T(8,128)(2,1)} %k_hbm.1, bf16[1,128,384]{2,1,0:T(8,128)(2,1)} %v_hbm.1, s32[1,3,2,16]{3,2,1,0:T(2,128)} %lists.1, s32[1,2,3]{2,1,0:T(2,128)} %bitcast.1, bf16[384,768]{1,0:T(8,128)(2,1)} %w_hbm.1), custom_call_target="tpu_custom_call" | custom-call | tf_op jit(solution)/shard_map/attention/pallas_call | solution.py:410
  68.6 1.5 %copy.8 = bf16[4,16,768]{2,1,0:T(8,128)(2,1)} copy(bf16[4,16,768]{2,1,0:T(8,128)(2,1)} %attention.1) | data formatting | bytes 196608

commit v3 on v2

--- a/solution.py
+++ b/solution.py
@@ -31,8 +31,7 @@
     t_all,
     t_wide,
     hot,
-    k_all,
-    v_all,
+    kv_all,
     v_stage,
     top_now,
     sum_now,
@@ -65,6 +64,7 @@
     w_recv,
     r_send,
     r_recv,
+    word,
 ):
     nx, ny, nz, nd = sizes
     heads, rows = q_hbm.shape[2] // HD, q_hbm.shape[1]
@@ -83,6 +83,20 @@
     def at_z(step):
         return {"uly": lax.rem(z + step + nz, nz) * 2 + core}
 
+    def at_ring(step):
+        place = lax.rem(d * nz + z + step + nd * nz, nd * nz)
+        return {"uly": lax.rem(place, nz) * 2 + core, "dp": place // nz}
+
+    def pass_word(turn):
+        if turn:
+            pl.semaphore_wait(word.at[turn - 1, 0], 1)
+            pl.semaphore_wait(word.at[turn - 1, 1], 1)
+        if turn < nz:
+            for way, device in enumerate(beside):
+                pl.semaphore_signal(
+                    word.at[turn, way], inc=1, device_id=device, device_id_type=MESH
+                )
+
     def at_a(flip, step):
         return {
             "uly": z * 2 + lax.rem(core + flip, 2),
@@ -99,14 +113,16 @@
             device_id_type=MESH,
         )
 
-    def kv_copy(h, way, step, which):
-        buffer = (k_all, v_all)[which]
+    def kv_copy(h, way, step):
         old, new = (step - 1, step) if way == 0 else ((ny - step + 1) % ny, ny - step)
-        return send(
-            buffer.at[h, old],
-            buffer.at[h, new],
-            kv_send.at[h, way, step - 1, which],
-            kv_recv.at[h, new, which],
+        src, dst = kv_all.at[h, old], kv_all.at[h, new]
+        if step == far:
+            src, dst = kv_all.at[h, old, way], kv_all.at[h, new, way]
+        return send(
+            src,
+            dst,
+            kv_send.at[h, way, step - 1],
+            kv_recv.at[h, new if (way, step) != (1, far) else ny],
             at_y(1 - 2 * way),
         )
 
@@ -176,21 +192,13 @@
         copy.start()
         started.append(copy)
 
-    def ways(step):
-        pairs = []
-        for which in range(2):
-            for way in range(2):
-                if step < far or which == way:
-                    pairs.append((way, which))
-        return pairs
-
     def load(src, dst, sem):
         copy = pltpu.make_async_copy(src, dst, sem)
         copy.start()
         return copy
 
     load_k = [
-        load(k_hbm.at[0, :, pl.ds(h * HD, HD)], k_all.at[h, 0], load_sem.at[0, h])
+        load(k_hbm.at[0, :, pl.ds(h * HD, HD)], kv_all.at[h, 0, 0], load_sem.at[0, h])
         for h in range(heads)
     ]
     load_v = [
@@ -210,12 +218,13 @@
         for h in range(heads)
     ]
 
+    beside = [at_ring(1), at_ring(-1)] if nz * nd > 1 else []
     barrier = pltpu.get_barrier_semaphore()
     around = [at_y(1), at_y(-1)]
     around += [at_x(j) for j in range(1, nx)]
     near = sorted({1 % nd, nd - 1} - {0})
-    around += [at_a(f, s) for s in [0] + near for f in range(2) if f or s]
-    around += [at_z(j) for j in range(1, nz)]
+    around += [at_a(1, 0)]
+    around += beside
     for device in around:
         pl.semaphore_signal(barrier, inc=1, device_id=device, device_id_type=MESH)
 
@@ -233,19 +242,27 @@
     for copy in load_k:
         copy.wait()
     load_v[0].wait()
-    v_all[0, 0] = v_stage[0].T
+    kv_all[0, 0, 1] = v_stage[0].T
     load_q[0].wait()
     pl.semaphore_wait(barrier, len(around))
 
-    for way, which in ways(1):
-        start(kv_copy(0, way, 1, which))
-    load_v[1].wait()
-    v_all[1, 0] = v_stage[1].T
-    for way, which in ways(1):
-        start(kv_copy(1, way, 1, which))
+    for way in range(2):
+        start(kv_copy(0, way, 1))
     for j in range(1, nx):
         start(t_copy(j))
         start(q_copy(0, j))
+
+    for h in range(1, heads):
+        load_v[h].wait()
+        kv_all[h, 0, 1] = v_stage[h].T
+        for way in range(2):
+            start(kv_copy(h, way, 1))
+    for h in range(1, heads):
+        load_q[h].wait()
+        for j in range(1, nx):
+            start(q_copy(h, j))
+    for h in range(heads):
+        start(w_copy(h))
 
     row = lax.broadcasted_iota(jnp.int32, (rows, HD), 0)
     column = lax.broadcasted_iota(jnp.int32, (rows, HD), 1)
@@ -253,16 +270,6 @@
     for s in range(ny):
         owner = lax.rem(y - s + ny, ny) * nx + x
         hot[s] = jnp.where(column == owner * per + row // BLOCK, 1.0, 0.0).astype(BF16)
-
-    for h in range(1, heads):
-        if h > 1:
-            load_v[h].wait()
-            v_all[h, 0] = v_stage[h].T
-        load_q[h].wait()
-        for j in range(1, nx):
-            start(q_copy(h, j))
-    for h in range(heads):
-        start(w_copy(h))
 
     for j in range(1, nx):
         t_copy(j).wait_recv()
@@ -275,9 +282,9 @@
 
     def attend(h, slots, first):
         keys = jnp.concatenate(
-            [jnp.concatenate([k_all[h, s], hot[s]], axis=1) for s in slots], axis=0
-        )
-        values = jnp.concatenate([v_all[h, s] for s in slots], axis=1)
+            [jnp.concatenate([kv_all[h, s, 0], hot[s]], axis=1) for s in slots], axis=0
+        )
+        values = jnp.concatenate([kv_all[h, s, 1] for s in slots], axis=1)
         queries = jnp.concatenate(
             [q_all[h].reshape(nx * rows, HD), t_wide[h].reshape(nx * rows, HD)], axis=1
         )
@@ -347,32 +354,27 @@
                 start(a_relay(h, flip))
 
     def receive_keys(h, step):
-        for way, which in ways(step):
-            kv_copy(h, way, step, which).wait_recv()
-            if step < far and (way, which) in ways(step + 1):
-                start(kv_copy(h, way, step + 1, which))
+        for way in range(2):
+            kv_copy(h, way, step).wait_recv()
+            if step < far:
+                start(kv_copy(h, way, step + 1))
 
     last = heads - 1
-    events = sorted((h + step, -h, step) for h in range(heads) for step in range(1, far + 1))
-    for _, h, step in events:
-        h = -h
+    events = [(h, step) for step in range(1, far + 1) for h in range(heads)]
+    for n, (h, step) in enumerate(events):
         receive_keys(h, step)
+        if beside and n % 2 == 0 and n // 2 <= nz:
+            pass_word(n // 2)
         if step == 1:
-            if h + 2 < heads:
-                for way, which in ways(1):
-                    start(kv_copy(h + 2, way, 1, which))
             for j in range(1, nx):
                 q_copy(h, j).wait_recv()
         slots = [0] * (step == 1) + ([step, ny - step] if step < far else [far])
         attend(h, slots, step == 1)
         if step == far:
             share(h)
-        if (h, step) == (last, far - 1):
-            merge(0)
-    for h in range(1, heads):
+    for h in range(heads):
         merge(h)
-    for h in range(heads):
-        relay(h)
+    relay(0)
     for h in range(heads):
         load_w[h].wait()
         w_copy(h).wait_recv()
@@ -380,6 +382,9 @@
     lines, depth = nz * take, heads * 2 * HD
     weights = w_all[...].reshape(depth, w_all.shape[2])
     for step in [0] + near + list(range(2, nd - 1)):
+        if near and step == near[0]:
+            for h in range(1, heads):
+                relay(h)
         for h in range(heads):
             for flip in range(2):
                 receive(h, flip, step)
@@ -419,8 +424,7 @@
             pltpu.VMEM((nx, 8, HD), F32),
             pltpu.VMEM((heads, nx, rows, HD), BF16),
             pltpu.VMEM((ny, rows, HD), BF16),
-            pltpu.VMEM((heads, ny, rows, HD), BF16),
-            pltpu.VMEM((heads, ny, HD, rows), BF16),
+            pltpu.VMEM((heads, ny, 2, rows, HD), BF16),
             pltpu.VMEM((heads, rows, HD), BF16),
             pltpu.VMEM((heads, 1, nx * rows), F32),
             pltpu.VMEM((heads, 1, nx * rows), F32),
@@ -437,8 +441,8 @@
             pltpu.VMEM((nz, nd, take, width), BF16),
             pltpu.VMEM((nz, nd, take, width), BF16),
             dma((4, heads)),
-            dma((heads, 2, far, 2)),
-            dma((heads, ny, 2)),
+            dma((heads, 2, far)),
+            dma((heads, ny + 1)),
             dma((heads, nx)),
             dma((heads, nx)),
             dma((nx,)),
@@ -453,6 +457,7 @@
             dma((heads,)),
             dma((nz, nd)),
             dma((nz, nd)),
+            pltpu.SemaphoreType.REGULAR((nz, 2)),
         ],
         compiler_params=pltpu.CompilerParams(
             collective_id=0, has_side_effects=True, vmem_limit_bytes=60 * 2**20

time: 70.3 us -> 66.3 us (0.943)
  Pallas kernels: 68.6 us -> 64.6 us
    pallas_call x1, Pallas kernels: 68.6 us -> 64.6 us  [on_device(): pl.pallas_call(functools.partial(fused, sizes), out_shape=jax.ShapeDtypeS...]
where the time goes in v3:
time: 66.3 us; the launch traced here: 66.1 us
  Pallas kernels  64.6 us (97%)
  local copies, waits for them, and re-layouts  1.54 us (2%)
    pallas_call x1, Pallas kernels, on_device(): pl.pallas_call(functools.partial(fused, sizes), out_shape=jax.ShapeDtypeS...  64.6 us
    unnamed x1, local copies, waits for them, and re-layouts  1.54 us

profile of v3, /device:TPU:1, one launch (start us, length us, event | category | flops | bytes accessed | tf_op | source)
XLA Modules:
  0.0 66.1 jit_solution(5850368687662280555)
XLA Ops:
  0.0 64.6 %attention.1 = bf16[4,16,768]{2,1,0:T(8,128)(2,1)} custom-call(bf16[1,128,384]{2,1,0:T(8,128)(2,1)} %q_hbm.1, bf16[1,128,384]{2,1,0:T(8,128)(2,1)} %k_hbm.1, bf16[1,128,384]{2,1,0:T(8,128)(2,1)} %v_hbm.1, s32[1,3,2,16]{3,2,1,0:T(2,128)} %lists.1, s32[1,2,3]{2,1,0:T(2,128)} %bitcast.1, bf16[384,768]{1,0:T(8,128)(2,1)} %w_hbm.1), custom_call_target="tpu_custom_call" | custom-call | tf_op jit(solution)/shard_map/attention/pallas_call | solution.py:415
  64.6 1.5 %copy.8 = bf16[4,16,768]{2,1,0:T(8,128)(2,1)} copy(bf16[4,16,768]{2,1,0:T(8,128)(2,1)} %attention.1) | data formatting | bytes 196608

commit v4 on v3

--- a/solution.py
+++ b/solution.py
@@ -40,7 +40,6 @@
     o_out,
     o_in,
     st_out,
-    st_in,
     a_out,
     a_all,
     w_all,
@@ -56,8 +55,6 @@
     t_recv,
     o_send,
     o_recv,
-    st_send,
-    st_recv,
     a_send,
     a_recv,
     w_send,
@@ -137,15 +134,6 @@
     def o_copy(h, j):
         return send(
             o_out.at[h, j], o_in.at[h, j], o_send.at[h, j], o_recv.at[h, j], at_x(-j)
-        )
-
-    def st_copy(h, j):
-        return send(
-            st_out.at[h, j],
-            st_in.at[h, j],
-            st_send.at[h, j],
-            st_recv.at[h, j],
-            at_x(-j),
         )
 
     def a_copy(h, flip, step):
@@ -309,27 +297,35 @@
     def share(h):
         for j in range(nx):
             lanes = slice(j * rows, (j + 1) * rows)
-            st_out[h, j, 0:1, :] = top_now[h, :, lanes]
-            st_out[h, j, 1:2, :] = sum_now[h, :, lanes]
             if j == 0:
+                st_out[h, j, 0:1, :] = top_now[h, :, lanes]
+                st_out[h, j, 1:2, :] = sum_now[h, :, lanes]
                 o_own[h] = acc[h, :, lanes]
             else:
-                o_out[h, j] = acc[h, :, lanes].astype(BF16)
-                start(st_copy(h, j))
+                o_out[h, j, 0:HD] = acc[h, :, lanes].astype(BF16)
+                line = lax.broadcasted_iota(jnp.int32, (16, rows), 0)
+                packed = jnp.zeros((16, rows), F32)
+                for k, rest in enumerate((top_now[h, :, lanes], sum_now[h, :, lanes])):
+                    for i in range(3):
+                        term = rest.astype(BF16).astype(F32)
+                        packed = jnp.where(line == 3 * k + i, term, packed)
+                        rest = rest - term
+                o_out[h, j, HD : HD + 16] = packed.astype(BF16)
                 start(o_copy(h, j))
 
     def merge(h):
+        tops, sums = [st_out[h, 0, 0:1, :]], [st_out[h, 0, 1:2, :]]
         for j in range(1, nx):
-            st_copy(h, j).wait_recv()
-        tops = [st_out[h, 0, 0:1, :]] + [st_in[h, j, 0:1, :] for j in range(1, nx)]
-        sums = [st_out[h, 0, 1:2, :]] + [st_in[h, j, 1:2, :] for j in range(1, nx)]
+            o_copy(h, j).wait_recv()
+            packed = o_in[h, j, HD : HD + 16].astype(F32)
+            tops.append(packed[0:1] + packed[1:2] + packed[2:3])
+            sums.append(packed[3:4] + packed[4:5] + packed[5:6])
         top = functools.reduce(jnp.maximum, tops)
         weights = [jnp.exp2((t - top) * SCALE) for t in tops]
         denom = sum(w * s for w, s in zip(weights, sums))
         total = o_own[h] * weights[0]
         for j in range(1, nx):
-            o_copy(h, j).wait_recv()
-            total = total + o_in[h, j].astype(F32) * weights[j]
+            total = total + o_in[h, j, 0:HD].astype(F32) * weights[j]
         attended = (total / denom).T.astype(BF16)
         for i in range(2 * nz):
             place = slice(i // 2 * take, (i // 2 + 1) * take)
@@ -430,9 +426,8 @@
             pltpu.VMEM((heads, 1, nx * rows), F32),
             pltpu.VMEM((heads, HD, nx * rows), F32),
             pltpu.VMEM((heads, HD, rows), F32),
-            pltpu.VMEM((heads, nx, HD, rows), BF16),
-            pltpu.VMEM((heads, nx, HD, rows), BF16),
-            pltpu.VMEM((heads, nx, 8, rows), F32),
+            pltpu.VMEM((heads, nx, HD + 16, rows), BF16),
+            pltpu.VMEM((heads, nx, HD + 16, rows), BF16),
             pltpu.VMEM((heads, nx, 8, rows), F32),
             pltpu.VMEM((heads, 2, nz * take, HD), BF16),
             pltpu.VMEM((heads, nd, nz * take, 2 * HD), BF16),
@@ -447,8 +442,6 @@
             dma((heads, nx)),
             dma((nx,)),
             dma((nx,)),
-            dma((heads, nx)),
-            dma((heads, nx)),
             dma((heads, nx)),
             dma((heads, nx)),
             dma((heads, 2, nd)),

time: 66.3 us -> 66.1 us (level)
  no operation moved by 1% of the time
where the time goes in v4:
time: 66.1 us; the launch traced here: 65.9 us
  Pallas kernels  64.3 us (97%)
  local copies, waits for them, and re-layouts  1.54 us (2%)
    pallas_call x1, Pallas kernels, on_device(): pl.pallas_call(functools.partial(fused, sizes), out_shape=jax.ShapeDtypeS...  64.3 us
    unnamed x1, local copies, waits for them, and re-layouts  1.54 us

profile of v4, /device:TPU:1, one launch (start us, length us, event | category | flops | bytes accessed | tf_op | source)
XLA Modules:
  0.0 65.9 jit_solution(18281794293812836262)
XLA Ops:
  0.0 64.3 %attention.1 = bf16[4,16,768]{2,1,0:T(8,128)(2,1)} custom-call(bf16[1,128,384]{2,1,0:T(8,128)(2,1)} %q_hbm.1, bf16[1,128,384]{2,1,0:T(8,128)(2,1)} %k_hbm.1, bf16[1,128,384]{2,1,0:T(8,128)(2,1)} %v_hbm.1, s32[1,3,2,16]{3,2,1,0:T(2,128)} %lists.1, s32[1,2,3]{2,1,0:T(2,128)} %bitcast.1, bf16[384,768]{1,0:T(8,128)(2,1)} %w_hbm.1), custom_call_target="tpu_custom_call" | custom-call | tf_op jit(solution)/shard_map/attention/pallas_call | solution.py:411
  64.3 1.5 %copy.8 = bf16[4,16,768]{2,1,0:T(8,128)(2,1)} copy(bf16[4,16,768]{2,1,0:T(8,128)(2,1)} %attention.1) | data formatting | bytes 196608
